TPU v7x, 32 devices: a whole 2x2x4 slice. The times are simulated.
32 devices in a mesh: pipe: 4 (over z), tensor: 4 (over y, core), feat: 2 (over x).
Axes of the slice: x: 2, y: 2, z: 4, core: 2. Of those that a mesh axis runs over, the one named last changes fastest.
Arguments:
- cotangent: bfloat16 [256, 3584], P('feat', 'tensor'), may hold values from -6 to 6
- resid_in: bfloat16 [4, 256, 3584], P('pipe', 'feat', 'tensor'), may hold values from -6 to 6
- gate_pre: bfloat16 [4, 256, 7168], P('pipe', None, 'feat'), may hold values from -6 to 6
- up_pre: bfloat16 [4, 256, 7168], P('pipe', None, 'feat'), may hold values from -6 to 6
- w_gate: bfloat16 [4, 3584, 7168], P('pipe', 'tensor', 'feat'), may hold values from -0.09375 to 0.09375
- w_up: bfloat16 [4, 3584, 7168], P('pipe', 'tensor', 'feat'), may hold values from -0.09375 to 0.09375
- w_down: bfloat16 [4, 7168, 3584], P('pipe', 'feat', 'tensor'), may hold values from -0.0625 to 0.0625
- norm_gain: float32 [4, 3584], P('pipe', 'tensor'), may hold values from 0.25 to 1.75
- decoder: bfloat16 [4, 65536, 3584], P('pipe', 'feat', 'tensor'), may hold values from -0.09375 to 0.09375
- latent_ids: int32 [4, 256, 32], P('pipe'), may hold values from 0 to 65535
- latent_vals: float32 [4, 256, 32], P('pipe'), may hold values from 0.5 to 8
- attention_mask: int32 [256], replicated, may hold values from 0 to 1, as said below
Outputs:
- attribution: float32 [4, 65536], P('pipe', 'feat')
Inputs may be any that keep to these rules, and one draw needn't show every extreme that they name: `attention_mask`: each of the 2 contexts of 128 tokens is live on a prefix; the first context is live throughout, every other one on 64 to 127 tokens.
All inputs are finite; a program needn't handle non-finite values.
Results may differ from a plain program's by a relative error of at most 0.015.
Values may be sent and summed in bfloat16 or wider, within the bound.
A program may use at most 320 MiB of HBM per device.

v0:
```python
import jax
import jax.numpy as jnp
from jax import lax
from jax.sharding import PartitionSpec as P

EPS = 1e-06


def passed_along(value, axis, steps):
    count = lax.axis_size(axis)
    first, last = (max(0, -steps), min(count, count - steps))
    return lax.ppermute(value, axis, [(source, source + steps) for source in range(first, last)])


def gelu_pair(pre_act):
    return jax.vjp(lambda value: jax.nn.gelu(value, approximate=True), pre_act)


def layer_backward(grads, resid_own, gate, upper, w_gate, w_up, w_down, gain, feat_idx, row_share):
    width = grads.shape[1] * lax.axis_size("tensor")
    partial_hidden = lax.dot_general(
        grads, w_down, (((1,), (1,)), ((), ())), preferred_element_type=jnp.float32
    )
    hidden_grad = lax.psum(partial_hidden, "tensor")
    active, pullback = gelu_pair(gate.astype(jnp.float32))
    gate_grad = pullback(hidden_grad * upper.astype(jnp.float32))[0].astype(jnp.bfloat16)
    up_grad = (hidden_grad * active).astype(jnp.bfloat16)
    first = lax.dot_general(
        gate_grad, w_gate, (((1,), (1,)), ((), ())), preferred_element_type=jnp.float32
    )
    second = lax.dot_general(
        up_grad, w_up, (((1,), (1,)), ((), ())), preferred_element_type=jnp.float32
    )
    normed_grad = lax.psum_scatter(first + second, "feat", scatter_dimension=0, tiled=True)
    resid_f = resid_own.astype(jnp.float32)
    sq_part = jnp.sum(resid_f * resid_f, axis=1, keepdims=True)
    inner_part = jnp.sum(normed_grad * gain * resid_f, axis=1, keepdims=True)
    sq_sum, inner = lax.psum((sq_part, inner_part), "tensor")
    scale = lax.rsqrt(sq_sum / width + EPS)
    grads_own = lax.dynamic_slice_in_dim(grads, feat_idx * row_share, row_share, 0).astype(
        jnp.float32
    )
    result = (
        grads_own + gain * scale * normed_grad - resid_f * (scale * scale * scale) * inner / width
    )
    return lax.all_gather(result.astype(jnp.bfloat16), "feat", axis=0, tiled=True)


def on_device(
    cotangent,
    resid_in,
    gate_pre,
    up_pre,
    w_gate,
    w_up,
    w_down,
    norm_gain,
    decoder,
    latent_ids,
    latent_vals,
    attention_mask,
):
    feat_size = lax.axis_size("feat")
    pipe_size = lax.axis_size("pipe")
    section_idx = lax.axis_index("pipe")
    feat_idx = lax.axis_index("feat")
    cot_whole = lax.all_gather(cotangent, "feat", axis=0, tiled=True)
    tokens = gate_pre.shape[1]
    width_dev = cotangent.shape[1]
    pieces = 1
    row_share = tokens // (feat_size * pieces)

    def take_piece(whole_rows, step_piece):
        shaped = whole_rows.reshape(feat_size, pieces, row_share, whole_rows.shape[-1])
        picked = lax.dynamic_index_in_dim(shaped, step_piece, 1, keepdims=False)
        return picked.reshape(feat_size * row_share, whole_rows.shape[-1])

    resid_pieces = resid_in[0].reshape(pieces, row_share, width_dev)
    grad_store = jnp.zeros((feat_size, pieces, row_share, width_dev), jnp.bfloat16)
    received = jnp.zeros((feat_size * row_share, width_dev), jnp.bfloat16)
    is_top = section_idx == pipe_size - 1
    total_steps = pipe_size + pieces - 1
    for step in range(total_steps):
        piece_raw = step - (pipe_size - 1 - section_idx)
        is_valid = (piece_raw >= 0) & (piece_raw < pieces)
        step_piece = jnp.clip(piece_raw, 0, pieces - 1)
        incoming = jnp.where(is_top, take_piece(cot_whole, step_piece), received)
        resid_own = lax.dynamic_index_in_dim(resid_pieces, step_piece, 0, keepdims=False)
        outgoing = layer_backward(
            incoming,
            resid_own,
            take_piece(gate_pre[0], step_piece),
            take_piece(up_pre[0], step_piece),
            w_gate[0],
            w_up[0],
            w_down[0],
            norm_gain[0],
            feat_idx,
            row_share,
        )
        updated = lax.dynamic_update_index_in_dim(
            grad_store, outgoing.reshape(feat_size, 1, row_share, width_dev), step_piece, 1
        )
        grad_store = jnp.where(is_valid, updated, grad_store)
        if step + 1 < total_steps:
            received = passed_along(outgoing, "pipe", -1)
    layer_grads = grad_store.reshape(tokens, width_dev)
    lat_dev = decoder.shape[1]
    local_ix = latent_ids[0] - feat_idx * lat_dev
    inside = (local_ix >= 0) & (local_ix < lat_dev)
    live = attention_mask.astype(jnp.float32)
    act_weights = jnp.where(inside, latent_vals[0] * live[:, None], 0.0)
    slot_ix = jnp.clip(local_ix, 0, lat_dev - 1)
    token_ix = jnp.broadcast_to(jnp.arange(tokens, dtype=jnp.int32)[:, None], slot_ix.shape)
    dense_acts = jnp.zeros((tokens, lat_dev), jnp.float32).at[token_ix, slot_ix].add(act_weights)
    scores = lax.dot_general(
        layer_grads, decoder[0], (((1,), (1,)), ((), ())), preferred_element_type=jnp.float32
    )
    partial_value = jnp.sum(dense_acts * scores, axis=0)
    attribution = lax.psum(partial_value, "tensor")
    return attribution[None, :]


def solution(mesh):
    return jax.shard_map(
        on_device,
        mesh=mesh,
        in_specs=(
            P("feat", "tensor"),
            P("pipe", "feat", "tensor"),
            P("pipe", None, "feat"),
            P("pipe", None, "feat"),
            P("pipe", "tensor", "feat"),
            P("pipe", "tensor", "feat"),
            P("pipe", "feat", "tensor"),
            P("pipe", "tensor"),
            P("pipe", "feat", "tensor"),
            P("pipe", None, None),
            P("pipe", None, None),
            P(),
        ),
        out_specs=P("pipe", "feat"),
        check_vma=False,
    )
```

profile of v0, /device:TPU:0, one launch (start us, length us, event | category | flops | bytes accessed | tf_op | source)
XLA Modules:
  0.0 737.2 jit_solution(7225823080701337240)
XLA Ops:
  6.5 9.5 %all_gather.15 = bf16[256,896]{1,0:T(8,128)(2,1)S(1)} all-gather(bf16[128,896]{1,0:T(8,128)(2,1)} %param.12), channel_id=1, replica_groups=mesh['pipe'=4,'tensor'=4,'feat'=2] {'feat'}, dimensions={0}, use_global_device_ids=true | all-gather | bytes 688128 | tf_op jit(solution)/shard_map/all_gather | solution.py:67
  16.0 6.8 fusion.29
  22.9 78.5 %all-reduce.7.cloned.1.call-done = f32[256,3584]{1,0:T(8,128)} async-done(((f32[256,3584]{1,0:T(8,128)}), f32[256,3584]{1,0:T(8,128)}) %all-reduce.7.cloned.1.call-update) | async-done | bytes 3670032 | tf_op jit(solution)/shard_map/psum | solution.py:24
  101.4 6.6 fusion.13
  108.1 7.8 %fusion.94 = f32[256,896]{1,0:T(8,128)} fusion(f32[256,896]{1,0:T(8,128)S(1)} %fusion.13, bf16[1,896,3584]{2,1,0:T(8,128)(2,1)} %param.16, f32[256,3584]{1,0:T(8,128)S(1)} %copy-done.7, bf16[1,256,3584]{2,1,0:T(8,128)(2,1)S(1)} %copy-done.14, bf16[1,256,3584]{2,1,0:T(8,128)(2,1)S(1)} %copy-done.11), kind=kOutput, calls=%fused_computation.105 | convolution fusion | flops 1665499136 | bytes 15597568 | tf_op jit(solution)/shard_map/dot_general | solution.py:28
  116.0 19.1 %reduce-scatter.5.cloned.1.call-done = f32[128,896]{1,0:T(8,128)} async-done(((f32[256,896]{1,0:T(8,128)}), f32[128,896]{1,0:T(8,128)}) %reduce-scatter.5.cloned.1.call-update) | async-done | bytes 458768 | tf_op jit(solution)/shard_map/reduce_scatter | solution.py:34
  135.1 1.2 fusion.130
  136.3 6.9 all-reduce
  143.1 1.2 fusion.120
  144.4 6.9 all_gather.16
  151.2 1.3 collective-permute-start
  152.5 10.8 %collective-permute-done = bf16[256,896]{1,0:T(8,128)(2,1)S(1)} collective-permute-done((bf16[256,896]{1,0:T(8,128)(2,1)S(1)}, bf16[256,896]{1,0:T(8,128)(2,1)S(1)}, u32[]{:S(2)}, u32[]{:S(2)}) %collective-permute-start) | collective-permute-done | bytes 458784 | tf_op jit(solution)/shard_map/ppermute | solution.py:12
  163.4 6.8 fusion.27
  170.4 77.0 %all-reduce.9.cloned.1.call-done = f32[256,3584]{1,0:T(8,128)} async-done(((f32[256,3584]{1,0:T(8,128)}), f32[256,3584]{1,0:T(8,128)}) %all-reduce.9.cloned.1.call-update) | async-done | bytes 3670032 | tf_op jit(solution)/shard_map/psum | solution.py:24
  247.4 7.1 fusion.11
  254.5 8.8 %fusion.99 = f32[256,896]{1,0:T(8,128)} fusion(f32[256,896]{1,0:T(8,128)S(1)} %fusion.11, bf16[1,896,3584]{2,1,0:T(8,128)(2,1)} %param.16, f32[256,3584]{1,0:T(8,128)S(1)} %copy-done.8, bf16[1,256,3584]{2,1,0:T(8,128)(2,1)} %param.15, bf16[1,256,3584]{2,1,0:T(8,128)(2,1)} %param.14), kind=kOutput, calls=%fused_computation.106 | convolution fusion | flops 1665499136 | bytes 15597568 | tf_op jit(solution)/shard_map/dot_general | solution.py:28
  263.4 19.1 %reduce-scatter.7.cloned.1.call-done = f32[128,896]{1,0:T(8,128)} async-done(((f32[256,896]{1,0:T(8,128)}), f32[128,896]{1,0:T(8,128)}) %reduce-scatter.7.cloned.1.call-update) | async-done | bytes 458768 | tf_op jit(solution)/shard_map/reduce_scatter | solution.py:34
  282.5 1.2 fusion.132
  283.6 6.9 psum.83
  290.5 1.2 fusion.123
  291.8 6.8 all_gather.17
  298.6 1.3 collective-permute-start.1
  299.9 10.7 %collective-permute-done.1 = bf16[256,896]{1,0:T(8,128)(2,1)S(1)} collective-permute-done((bf16[256,896]{1,0:T(8,128)(2,1)S(1)}, bf16[256,896]{1,0:T(8,128)(2,1)S(1)}, u32[]{:S(2)}, u32[]{:S(2)}) %collective-permute-start.1) | collective-permute-done | bytes 458784 | tf_op jit(solution)/shard_map/ppermute | solution.py:12
  310.7 6.8 fusion.25
  317.7 77.1 %all-reduce.11.cloned.1.call-done = f32[256,3584]{1,0:T(8,128)} async-done(((f32[256,3584]{1,0:T(8,128)}), f32[256,3584]{1,0:T(8,128)}) %all-reduce.11.cloned.1.call-update) | async-done | bytes 3670032 | tf_op jit(solution)/shard_map/psum | solution.py:24
  394.8 7.1 fusion.9
  401.9 7.7 %fusion.104 = f32[256,896]{1,0:T(8,128)} fusion(f32[256,896]{1,0:T(8,128)S(1)} %fusion.9, bf16[1,896,3584]{2,1,0:T(8,128)(2,1)} %param.16, f32[256,3584]{1,0:T(8,128)S(1)} %copy-done.9, bf16[1,256,3584]{2,1,0:T(8,128)(2,1)S(1)} %copy-done.15, bf16[1,256,3584]{2,1,0:T(8,128)(2,1)S(1)} %copy-done.12), kind=kOutput, calls=%fused_computation.107 | convolution fusion | flops 1665499136 | bytes 15597568 | tf_op jit(solution)/shard_map/dot_general | solution.py:28
  409.7 19.1 %reduce-scatter.9.cloned.1.call-done = f32[128,896]{1,0:T(8,128)} async-done(((f32[256,896]{1,0:T(8,128)}), f32[128,896]{1,0:T(8,128)}) %reduce-scatter.9.cloned.1.call-update) | async-done | bytes 458768 | tf_op jit(solution)/shard_map/reduce_scatter | solution.py:34
  428.8 1.2 fusion.133
  430.0 6.9 psum.85
  436.8 1.2 fusion.126
  438.1 6.9 all_gather.18
  444.9 1.3 collective-permute-start.2
  446.2 10.8 %collective-permute-done.2 = bf16[256,896]{1,0:T(8,128)(2,1)S(1)} collective-permute-done((bf16[256,896]{1,0:T(8,128)(2,1)S(1)}, bf16[256,896]{1,0:T(8,128)(2,1)S(1)}, u32[]{:S(2)}, u32[]{:S(2)}) %collective-permute-start.2) | collective-permute-done | bytes 458784 | tf_op jit(solution)/shard_map/ppermute | solution.py:12
  457.0 6.8 fusion.23
  463.8 0.3 reduce-scatter.11.cloned.1.call-start
  464.1 76.9 %all-reduce.13.cloned.1.call-done = f32[256,3584]{1,0:T(8,128)} async-done(((f32[256,3584]{1,0:T(8,128)}), f32[256,3584]{1,0:T(8,128)}) %all-reduce.13.cloned.1.call-update) | async-done | bytes 3670032 | tf_op jit(solution)/shard_map/psum | solution.py:24
  541.0 7.1 fusion.7
  548.2 7.8 %fusion.109 = f32[256,896]{1,0:T(8,128)} fusion(f32[256,896]{1,0:T(8,128)S(1)} %fusion.7, bf16[1,896,3584]{2,1,0:T(8,128)(2,1)} %param.16, f32[256,3584]{1,0:T(8,128)S(1)} %copy-done.10, bf16[1,256,3584]{2,1,0:T(8,128)(2,1)S(1)} %copy-done.16, bf16[1,256,3584]{2,1,0:T(8,128)(2,1)S(1)} %copy-done.13), kind=kOutput, calls=%fused_computation.108 | convolution fusion | flops 1665499136 | bytes 15597568 | tf_op jit(solution)/shard_map/dot_general | solution.py:28
  556.7 56.7 %scatter_custom_fusion = f32[8388608]{0:T(1024)} fusion(s32[8192]{0:T(1024)S(1)} %reshape.122, f32[8192]{0:T(1024)S(1)} %reshape.124, f32[]{:T(128)} %constant.95.clone.1), kind=kCustom, calls=%fused_computation.4 | custom fusion | flops 8192 | bytes 33554436
  613.4 35.9 %reshape.114 = f32[256,32768]{1,0:T(8,128)} reshape(f32[8388608]{0:T(1024)} %scatter_custom_fusion) | data formatting | bytes 67108864 | tf_op jit(solution)/shard_map/scatter-add | solution.py:115
  649.3 1.2 fusion.134
  650.5 5.8 psum.87
  656.3 1.2 fusion.129
  657.5 7.9 %all_gather.19 = bf16[256,896]{1,0:T(8,128)(2,1)S(1)} all-gather(bf16[128,896]{1,0:T(8,128)(2,1)S(1)} %fusion.129), channel_id=1, replica_groups=mesh['pipe'=4,'tensor'=4,'feat'=2] {'feat'}, dimensions={0}, use_global_device_ids=true | all-gather | bytes 688128 | tf_op jit(solution)/shard_map/all_gather | solution.py:46
  665.4 31.4 %fusion.31 = f32[32768]{0:T(1024)} fusion(f32[256,32768]{1,0:T(8,128)} %reshape.114, bf16[1,32768,896]{2,1,0:T(8,128)(2,1)} %param.20, bf16[256,896]{1,0:T(8,128)(2,1)S(1)} %all_gather.19, bf16[256,896]{1,0:T(8,128)(2,1)S(1)} %all_gather.18, bf16[256,896]{1,0:T(8,128)(2,1)S(1)} %all_gather.17, bf16[256,896]{1,0:T(8,128)(2,1)S(1)} %all_gather.16, ...), kind=kOutput, calls=%fused_computation.42 | convolution fusion | flops 15050047488 | bytes 94240768 | tf_op jit(solution)/shard_map/dot_general | solution.py:116
  696.9 31.7 %all-reduce.15.cloned.1.call-done = f32[1,32768]{1,0:T(1,128)} async-done(((f32[1,32768]{1,0:T(1,128)}), f32[1,32768]{1,0:T(1,128)}) %all-reduce.15.cloned.1.call-update) | async-done | bytes 131088 | tf_op jit(solution)/shard_map/psum | solution.py:120
  728.6 1.6 copy.21
  (69 shorter events, 1.7 us)
Async XLA Ops:
  6.5 94.9 %all-reduce.7.cloned.1.call-start = ((), (), s32[]{:S(2)}) async-start(), calls=%async_computation.4 | async-start | bytes 7340032 | tf_op jit(solution)/shard_map/psum | solution.py:24
  22.8 78.6 %copy-start.11 = (bf16[1,256,3584]{2,1,0:T(8,128)(2,1)S(1)}, bf16[1,256,3584]{2,1,0:T(8,128)(2,1)}, u32[]{:S(2)}) copy-start(bf16[1,256,3584]{2,1,0:T(8,128)(2,1)} %param.14) | copy-start | bytes 5505028
  22.8 112.2 %reduce-scatter.5.cloned.1.call-start = ((), (), s32[]{:S(2)}) async-start(), calls=%async_computation.5 | async-start | bytes 1376256 | tf_op jit(solution)/shard_map/reduce_scatter | solution.py:34
  101.4 6.7 copy-start.7
  101.4 6.7 copy-start.14
  108.1 7.9 %copy-start.3 = (f32[1,896]{1,0:T(1,128)S(1)}, f32[1,896]{1,0:T(1,128)}, u32[]{:S(2)}) copy-start(f32[1,896]{1,0:T(1,128)} %param.19) | copy-start | bytes 10756
  108.1 27.0 %copy-start = (bf16[1,128,896]{2,1,0:T(8,128)(2,1)S(1)}, bf16[1,128,896]{2,1,0:T(8,128)(2,1)}, u32[]{:S(2)}) copy-start(bf16[1,128,896]{2,1,0:T(8,128)(2,1)} %param.13) | copy-start | bytes 688132
  115.9 131.5 %all-reduce.9.cloned.1.call-start = ((), (), s32[]{:S(2)}) async-start(), calls=%async_computation.6 | async-start | bytes 7340032 | tf_op jit(solution)/shard_map/psum | solution.py:24
  151.2 12.1 %collective-permute-start = (bf16[256,896]{1,0:T(8,128)(2,1)S(1)}, bf16[256,896]{1,0:T(8,128)(2,1)S(1)}, u32[]{:S(2)}, u32[]{:S(2)}) collective-permute-start(bf16[256,896]{1,0:T(8,128)(2,1)S(1)} %all_gather.16), channel_id=1, source_target_pairs={{8,0},{16,8},{24,16},{9,1},{17,9},{25,17},{10,2},{18,10},{26,18},{... | collective-permute-start | bytes 1376264 | tf_op jit(solution)/shard_map/ppermute | solution.py:12
  170.1 112.3 %reduce-scatter.7.cloned.1.call-start = ((), (), s32[]{:S(2)}) async-start(), calls=%async_computation.7 | async-start | bytes 1376256 | tf_op jit(solution)/shard_map/reduce_scatter | solution.py:34
  247.4 7.1 copy-start.8
  263.3 131.4 %all-reduce.11.cloned.1.call-start = ((), (), s32[]{:S(2)}) async-start(), calls=%async_computation.8 | async-start | bytes 7340032 | tf_op jit(solution)/shard_map/psum | solution.py:24
  298.6 12.0 %collective-permute-start.1 = (bf16[256,896]{1,0:T(8,128)(2,1)S(1)}, bf16[256,896]{1,0:T(8,128)(2,1)S(1)}, u32[]{:S(2)}, u32[]{:S(2)}) collective-permute-start(bf16[256,896]{1,0:T(8,128)(2,1)S(1)} %all_gather.17), channel_id=1, source_target_pairs={{8,0},{16,8},{24,16},{9,1},{17,9},{25,17},{10,2},{18,10},{26,18},{... | collective-permute-start | bytes 1376264 | tf_op jit(solution)/shard_map/ppermute | solution.py:12
  317.4 111.4 %reduce-scatter.9.cloned.1.call-start = ((), (), s32[]{:S(2)}) async-start(), calls=%async_computation.9 | async-start | bytes 1376256 | tf_op jit(solution)/shard_map/reduce_scatter | solution.py:34
  394.8 7.1 copy-start.9
  394.8 7.1 copy-start.12
  394.8 7.1 copy-start.15
  409.7 131.3 %all-reduce.13.cloned.1.call-start = ((), (), s32[]{:S(2)}) async-start(), calls=%async_computation.10 | async-start | bytes 7340032 | tf_op jit(solution)/shard_map/psum | solution.py:24
  444.9 12.1 %collective-permute-start.2 = (bf16[256,896]{1,0:T(8,128)(2,1)S(1)}, bf16[256,896]{1,0:T(8,128)(2,1)S(1)}, u32[]{:S(2)}, u32[]{:S(2)}) collective-permute-start(bf16[256,896]{1,0:T(8,128)(2,1)S(1)} %all_gather.18), channel_id=1, source_target_pairs={{8,0},{16,8},{24,16},{9,1},{17,9},{25,17},{10,2},{18,10},{26,18},{... | collective-permute-start | bytes 1376264 | tf_op jit(solution)/shard_map/ppermute | solution.py:12
  463.8 185.5 %reduce-scatter.11.cloned.1.call-start = ((), (), s32[]{:S(2)}) async-start(), calls=%async_computation.11 | async-start | bytes 1376256 | tf_op jit(solution)/shard_map/reduce_scatter | solution.py:34
  541.0 7.1 copy-start.10
  541.0 7.1 copy-start.13
  541.0 7.1 copy-start.16
  548.1 7.9 %copy-start.1 = (s32[1,256,32]{1,2,0:T(8,128)S(1)}, s32[1,256,32]{1,2,0:T(8,128)}, u32[]{:S(2)}) copy-start(s32[1,256,32]{1,2,0:T(8,128)} %param.21) | copy-start | bytes 98308
  548.1 7.9 %copy-start.6 = (s32[2]{0:T(128)S(1)}, s32[2]{0:T(128)}, u32[]{:S(2)}) copy-start(s32[2]{0:T(128)} %constant.125) | copy-start | bytes 28
  548.1 8.0 %copy-start.5 = (s32[2]{0:T(128)S(1)}, s32[2]{0:T(128)}, u32[]{:S(2)}) copy-start(s32[2]{0:T(128)} %constant.128) | copy-start | bytes 28
  548.2 8.3 %copy-start.4 = (s32[256]{0:T(256)S(1)}, s32[256]{0:T(256)}, u32[]{:S(2)}) copy-start(s32[256]{0:T(256)} %param.23) | copy-start | bytes 3076
  548.2 8.3 %copy-start.2 = (f32[1,256,32]{1,2,0:T(8,128)S(1)}, f32[1,256,32]{1,2,0:T(8,128)}, u32[]{:S(2)}) copy-start(f32[1,256,32]{1,2,0:T(8,128)} %param.22) | copy-start | bytes 98308
  556.0 172.6 %all-reduce.15.cloned.1.call-start = ((), (), s32[]{:S(2)}) async-start(), calls=%async_computation.12 | async-start | bytes 262144 | tf_op jit(solution)/shard_map/psum | solution.py:120
Sparse Core Ops, SparseCore 0:
  22.9 78.3 all-reduce.6
  116.0 18.9 reduce-scatter.4
  170.3 77.0 all-reduce.8
  263.4 18.9 reduce-scatter.6
  317.6 77.1 all-reduce.10
  409.8 18.9 reduce-scatter.8
  463.9 77.0 all-reduce.12
  556.1 18.9 reduce-scatter.10
  697.0 31.5 all-reduce.14
where the time goes:
time: 746 us; the launch traced here: 737 us
  waiting for transfers between devices  431 us (58%)
  matrix products  118 us (16%)
  other arithmetic  66.7 us (9%)
  blocking collectives  64.3 us (9%)
  local copies, waits for them, and re-layouts  37.9 us (5%)
  between operations  14.1 us (2%)
    psum x4, waiting for transfers between devices, layer_backward(): hidden_grad = lax.psum(partial_hidden, 'tensor')  309 us
    reduce_scatter x4, waiting for transfers between devices, layer_backward(): lax.psum_scatter(first + second, 'feat', scatter_dimension=0, tiled=True)  57.2 us
    unnamed x5, other arithmetic  56.9 us
    scatter-add x1, local copies, waits for them, and re-layouts, on_device(): jnp.zeros((tokens, lat_dev), jnp.float32).at[token_ix, slot_ix]  35.9 us
    ppermute x3, waiting for transfers between devices, passed_along(): lax.ppermute(value, axis, [(source, source + steps) for source in range(f...  32.3 us
    dot_general x4, matrix products, layer_backward(): lax.dot_general(gate_grad, w_gate, (((1,), (1,)), ((), ())), preferred_el...  32.1 us
    psum x1, waiting for transfers between devices, on_device(): attribution = lax.psum(partial_value, 'tensor')  31.7 us
    dot_general x1, matrix products, on_device(): lax.dot_general(layer_grads, decoder[0], (((1,), (1,)), ((), ())), prefer...  31.4 us
  transfers between devices with their start and end apart: 12, of which 11 were waited for; matrix products, arithmetic and copies ran while one was open for 13% of the time, Pallas kernels for 0%

commit v1 on v0

--- a/solution.py
+++ b/solution.py
@@ -1,6 +1,10 @@
+import functools
+
 import jax
 import jax.numpy as jnp
 from jax import lax
+from jax.experimental import pallas as pl
+from jax.experimental.pallas import tpu as pltpu
 from jax.sharding import PartitionSpec as P
 
 EPS = 1e-06
@@ -121,9 +125,453 @@
     return attribution[None, :]
 
 
+NT = (((1,), (1,)), ((), ()))
+GROUP = 8
+SQRT_2_OVER_PI = 0.7978845608028654
+LO = 256
+HIS_PER_STEP = 8
+
+
+def chain_kernel(
+    pieces, width, cot, resid, gate, upper, wg, wu, wd, gain, out,
+    zin, resid_full, fac_gate, fac_up, s1, r1, acc, s2, r2, hid, nacc, sx, rx, msg_s, msg_r, res,
+    zin_send, zin_recv, rs_send, rs_recv, y_send, y_recv, ag_send, ag_recv,
+    x_send, x_recv, m_send, m_recv, z_send, resid_send, resid_recv,
+):
+    pipe, tensor, feat = lax.axis_index("pipe"), lax.axis_index("tensor"), lax.axis_index("feat")
+    pipe_size = lax.axis_size("pipe")
+    y, core = tensor // 2, lax.rem(tensor, 2)
+    is_top, is_bottom = pipe == pipe_size - 1, pipe == 0
+    tokens, ff = gate.shape
+    rows = tokens // pieces
+    own_rows = tokens // 2
+    own_pieces = pieces // 2
+    half = ff // 2
+    core_peer = {"tensor": y * 2 + (1 - core)}
+    y_peer = {"tensor": (1 - y) * 2 + core}
+    x_peer = {"feat": 1 - feat}
+    own_cols = pl.ds(pl.multiple_of(core * half, half), half)
+
+    def group_peer(j):
+        return {
+            "tensor": lax.rem(y + (j // 2) % 2, 2) * 2 + lax.rem(core + j % 2, 2),
+            "feat": lax.rem(feat + j // 4, 2),
+        }
+
+    def rows_of(p):
+        return pl.ds(pl.multiple_of(p * rows, rows), rows)
+
+    def send(src, dst, send_sem, recv_sem, device):
+        return pltpu.make_async_remote_copy(
+            src_ref=src, dst_ref=dst, send_sem=send_sem, recv_sem=recv_sem,
+            device_id=device, device_id_type=pl.DeviceIdType.MESH,
+        )
+
+    def cot_copy(p):
+        return send(zin.at[rows_of(p)], zin.at[rows_of(p)], zin_send.at[p], zin_recv.at[p], x_peer)
+
+    own_part = pl.ds(pl.multiple_of(feat * own_rows, own_rows), own_rows)
+
+    def resid_copy():
+        return send(
+            resid_full.at[own_part], resid_full.at[own_part],
+            resid_send.at[0], resid_recv.at[0], x_peer,
+        )
+
+    def other_resid():
+        part = pl.ds(pl.multiple_of((1 - feat) * own_rows, own_rows), own_rows)
+        return send(
+            resid_full.at[part], resid_full.at[part], resid_send.at[0], resid_recv.at[0], x_peer
+        )
+
+    def rs_copy(p):
+        return send(s1.at[rows_of(p)], r1.at[rows_of(p)], rs_send.at[p], rs_recv.at[p], core_peer)
+
+    def y_copy(p):
+        return send(s2.at[rows_of(p)], r2.at[rows_of(p)], y_send.at[p], y_recv.at[p], y_peer)
+
+    def ag_copy(p):
+        part = hid.at[rows_of(p), own_cols]
+        return send(part, part, ag_send.at[p], ag_recv.at[p], core_peer)
+
+    def ag_arrival(p):
+        part = hid.at[
+            rows_of(p), pl.ds(pl.multiple_of((1 - core) * half, half), half)
+        ]
+        return send(part, part, ag_send.at[p], ag_recv.at[p], core_peer)
+
+    def x_copy(p):
+        return send(sx.at[rows_of(p)], rx.at[rows_of(p)], x_send.at[p], x_recv.at[p], x_peer)
+
+    def m_copy(p, j):
+        return send(
+            msg_s.at[p], msg_r.at[p, j - 1], m_send.at[p, j - 1], m_recv.at[p, j - 1], group_peer(j)
+        )
+
+    def z_copy(p):
+        return send(
+            res.at[rows_of(p)], zin.at[rows_of(p)], z_send.at[p], zin_recv.at[p],
+            {"pipe": jnp.maximum(pipe - 1, 0)},
+        )
+
+    barrier = pltpu.get_barrier_semaphore()
+    for j in range(1, GROUP):
+        pl.semaphore_signal(
+            barrier, inc=1, device_id=group_peer(j), device_id_type=pl.DeviceIdType.MESH
+        )
+
+    @pl.when(jnp.logical_not(is_top))
+    def _():
+        pl.semaphore_signal(
+            barrier, inc=1, device_id={"pipe": pipe + 1}, device_id_type=pl.DeviceIdType.MESH
+        )
+
+    @pl.when(jnp.logical_not(is_bottom))
+    def _():
+        pl.semaphore_signal(
+            barrier, inc=1, device_id={"pipe": pipe - 1}, device_id_type=pl.DeviceIdType.MESH
+        )
+
+    neighbours = GROUP - 1 + jnp.minimum(pipe_size - 1 - pipe, 1) + jnp.minimum(pipe, 1)
+    pl.semaphore_wait(barrier, neighbours)
+
+    @pl.when(is_top)
+    def _():
+        zin[own_part, :] = cot[...]
+        for i in range(own_pieces):
+            cot_copy(feat * own_pieces + i).start()
+
+    resid_full[own_part, :] = resid[...]
+    resid_copy().start()
+
+    def factors(p):
+        part = 512
+
+        @pl.loop(0, ff // part)
+        def _(n):
+            cols = pl.ds(pl.multiple_of(n * part, part), part)
+            g = gate[rows_of(p), cols].astype(jnp.float32)
+            u = upper[rows_of(p), cols].astype(jnp.float32)
+            th = jnp.tanh(SQRT_2_OVER_PI * (g + 0.044715 * (g * g * g)))
+            cdf = 0.5 * (1.0 + th)
+            slope = cdf + (0.5 * SQRT_2_OVER_PI) * g * (1.0 - th * th) * (
+                1.0 + (3.0 * 0.044715) * (g * g)
+            )
+            fac_gate[rows_of(p), cols] = slope * u
+            fac_up[rows_of(p), cols] = g * cdf
+
+    @pl.when(jnp.logical_not(is_top))
+    def _():
+        pl.loop(0, pieces)(factors)
+
+    tile = 256
+
+    def first_matmul(p):
+        @pl.when(jnp.logical_not(is_top) | (p // own_pieces != feat))
+        def _():
+            z_copy(p).wait_recv()
+
+        lhs = zin[rows_of(p), :]
+
+        @pl.loop(0, half // tile)
+        def _(n):
+            at = pl.multiple_of((1 - core) * half + n * tile, tile)
+            value = lax.dot_general(
+                lhs, wd[pl.ds(at, tile), :], NT, preferred_element_type=jnp.float32
+            )
+            s1[rows_of(p), pl.ds(pl.multiple_of(n * tile, tile), tile)] = value.astype(jnp.bfloat16)
+
+        rs_copy(p).start()
+
+        @pl.loop(0, half // tile)
+        def _(n):
+            at = pl.multiple_of(core * half + n * tile, tile)
+            acc[rows_of(p), pl.ds(pl.multiple_of(n * tile, tile), tile)] = lax.dot_general(
+                lhs, wd[pl.ds(at, tile), :], NT, preferred_element_type=jnp.float32
+            )
+
+        @pl.when(is_top)
+        def _():
+            factors(p)
+
+    def chip_sum(p):
+        rs_copy(p).wait_recv()
+        total = acc[rows_of(p), :] + r1[rows_of(p), :].astype(jnp.float32)
+        acc[rows_of(p), :] = total
+        s2[rows_of(p), :] = total.astype(jnp.bfloat16)
+        y_copy(p).start()
+
+    def pair_sum(p):
+        y_copy(p).wait_recv()
+        total = acc[rows_of(p), :] + r2[rows_of(p), :].astype(jnp.float32)
+        hid[rows_of(p), own_cols] = total.astype(jnp.bfloat16)
+        ag_copy(p).start()
+
+    def second_matmul(p):
+        ag_arrival(p).wait_recv()
+        part = 512
+        nacc[rows_of(p), :] = jnp.zeros((rows, nacc.shape[1]), jnp.float32)
+
+        @pl.loop(0, ff // part)
+        def _(n):
+            cols = pl.ds(pl.multiple_of(n * part, part), part)
+            h = hid[rows_of(p), cols].astype(jnp.float32)
+            gg = (h * fac_gate[rows_of(p), cols]).astype(jnp.bfloat16)
+            ug = (h * fac_up[rows_of(p), cols]).astype(jnp.bfloat16)
+            nacc[rows_of(p), :] += lax.dot_general(
+                gg, wg[:, cols], NT, preferred_element_type=jnp.float32
+            ) + lax.dot_general(ug, wu[:, cols], NT, preferred_element_type=jnp.float32)
+
+        part_sum = nacc[rows_of(p), :]
+        sx[rows_of(p), :] = part_sum.astype(jnp.bfloat16)
+        x_copy(p).start()
+        res_f = resid_full[rows_of(p), :].astype(jnp.float32)
+        inner = jnp.sum(part_sum * gain[...] * res_f, axis=1, keepdims=True)
+        sq = 0.5 * jnp.sum(res_f * res_f, axis=1, keepdims=True)
+        lane = lax.broadcasted_iota(jnp.int32, (rows, 128), 1)
+        both = jnp.where(lane < 4, inner, sq)
+        square = jnp.concatenate([both] * (128 // rows), axis=0)
+        msg_s[p] = square.T[:8, :]
+        for j in range(1, GROUP):
+            m_copy(p, j).start()
+
+    def finish(p):
+        for j in range(1, GROUP):
+            m_copy(p, j).wait_recv()
+        total = msg_s[p]
+        for j in range(1, GROUP):
+            total = total + msg_r[p, j - 1]
+        back = jnp.concatenate([total] * 16, axis=0).T
+        inner, sq_sum = back[:rows, 0:1], back[:rows, 4:5]
+        scale = lax.rsqrt(sq_sum / width + EPS)
+        x_copy(p).wait_recv()
+        normed = nacc[rows_of(p), :] + rx[rows_of(p), :].astype(jnp.float32)
+        res_f = resid_full[rows_of(p), :].astype(jnp.float32)
+        result = (
+            zin[rows_of(p), :].astype(jnp.float32)
+            + gain[...] * scale * normed
+            - res_f * ((scale * scale * scale) * inner / width)
+        ).astype(jnp.bfloat16)
+        res[rows_of(p), :] = result
+
+        @pl.when(jnp.logical_not(is_bottom))
+        def _():
+            z_copy(p).start()
+
+        out[rows_of(p), :] = result
+
+    @pl.loop(0, pieces + 2)
+    def _(s):
+        @pl.when(s < pieces)
+        def _():
+            first_matmul(s)
+
+        @pl.when(s >= 2)
+        def _():
+            finish(s - 2)
+
+        @pl.when((s >= 1) & (s <= pieces))
+        def _():
+            pair_sum(s - 1)
+
+        @pl.when(s < pieces)
+        def _():
+            chip_sum(s)
+
+        @pl.when(s == 1)
+        def _():
+            other_resid().wait_recv()
+
+        @pl.when((s >= 1) & (s <= pieces))
+        def _():
+            second_matmul(s - 1)
+
+    resid_copy().wait_send()
+
+    @pl.when(is_top)
+    def _():
+        for i in range(own_pieces):
+            cot_copy(feat * own_pieces + i).wait_send()
+
+    @pl.loop(0, pieces)
+    def _(p):
+        rs_copy(p).wait_send()
+        y_copy(p).wait_send()
+        ag_copy(p).wait_send()
+        x_copy(p).wait_send()
+        for j in range(1, GROUP):
+            m_copy(p, j).wait_send()
+
+        @pl.when(jnp.logical_not(is_bottom))
+        def _():
+            z_copy(p).wait_send()
+
+
+def chain(cotangent, resid, gate, upper, wg, wu, wd, gain):
+    pieces = 4
+    tokens, ff = gate.shape
+    width_dev = cotangent.shape[1]
+    half, rows = ff // 2, tokens // pieces
+    width = width_dev * lax.axis_size("tensor")
+    b16, f32 = jnp.bfloat16, jnp.float32
+    dma = pltpu.SemaphoreType.DMA
+    return pl.pallas_call(
+        functools.partial(chain_kernel, pieces, width),
+        out_shape=jax.ShapeDtypeStruct((tokens, width_dev), b16),
+        in_specs=[pl.BlockSpec(memory_space=pltpu.VMEM)] * 8,
+        out_specs=pl.BlockSpec(memory_space=pltpu.VMEM),
+        scratch_shapes=[
+            pltpu.VMEM((tokens, width_dev), b16),
+            pltpu.VMEM((tokens, width_dev), b16),
+            pltpu.VMEM((tokens, ff), f32),
+            pltpu.VMEM((tokens, ff), f32),
+            pltpu.VMEM((tokens, half), b16),
+            pltpu.VMEM((tokens, half), b16),
+            pltpu.VMEM((tokens, half), f32),
+            pltpu.VMEM((tokens, half), b16),
+            pltpu.VMEM((tokens, half), b16),
+            pltpu.VMEM((tokens, ff), b16),
+            pltpu.VMEM((tokens, width_dev), f32),
+            pltpu.VMEM((tokens, width_dev), b16),
+            pltpu.VMEM((tokens, width_dev), b16),
+            pltpu.VMEM((pieces, 8, 128), f32),
+            pltpu.VMEM((pieces, GROUP - 1, 8, 128), f32),
+            pltpu.VMEM((tokens, width_dev), b16),
+        ]
+        + [dma((pieces,))] * 10
+        + [dma((pieces, GROUP - 1))] * 2
+        + [dma((pieces,)), dma((1,)), dma((1,))],
+        compiler_params=pltpu.CompilerParams(
+            collective_id=0, has_side_effects=True, vmem_limit_bytes=58 * 2**20
+        ),
+        name="chain",
+    )(cotangent, resid, gate, upper, wg, wu, wd, gain)
+
+
+def score_kernel(grads, hi_ids, lo_ids, weights, dec, out, *dense):
+    tokens = grads.shape[0]
+    his = dense[0].shape[0] // tokens
+    slots = hi_ids.shape[1]
+
+    @pl.when(pl.program_id(0) == 0)
+    def _():
+        @pl.loop(0, tokens, unroll=4)
+        def _(t):
+            at = pl.ds(t, 1)
+            hi = lax.broadcasted_iota(jnp.int32, (his, slots), 0) == hi_ids[at, :]
+            lo = lax.broadcasted_iota(jnp.int32, (LO, slots), 0) == lo_ids[at, :]
+            lhs = jnp.where(hi, weights[at, :], 0.0).astype(jnp.bfloat16)
+            rhs = jnp.where(lo, 1.0, 0.0).astype(jnp.bfloat16)
+            value = lax.dot_general(lhs, rhs, NT, preferred_element_type=jnp.float32)
+            for n, ref in enumerate(dense):
+                ref[pl.ds(t, his, stride=tokens), :] = value[:, n * 128 : (n + 1) * 128]
+
+    first = pl.program_id(0) * HIS_PER_STEP
+    for j in range(HIS_PER_STEP):
+        scores = lax.dot_general(
+            grads[...], dec[j * LO : (j + 1) * LO, :], NT, preferred_element_type=jnp.float32
+        )
+        at = pl.ds(pl.multiple_of((first + j) * tokens, tokens), tokens)
+        for n, ref in enumerate(dense):
+            cols = slice(n * 128, (n + 1) * 128)
+            out[j : j + 1, cols] = jnp.sum(ref[at, :] * scores[:, cols], axis=0, keepdims=True)
+
+
+def score(grads, decoder, ids, weights):
+    tokens, width_dev = grads.shape
+    his = decoder.shape[0] // LO
+    coarse = weights.astype(jnp.bfloat16).astype(jnp.float32)
+    parts = jnp.concatenate([coarse, weights - coarse], axis=1)
+    both = jnp.concatenate([ids, ids], axis=1)
+    slots = both.shape[1]
+    fixed = lambda shape: pl.BlockSpec(shape, lambda i: (0, 0))
+    return pl.pallas_call(
+        score_kernel,
+        grid=(his // HIS_PER_STEP,),
+        out_shape=jax.ShapeDtypeStruct((his, LO), jnp.float32),
+        in_specs=[
+            fixed((tokens, width_dev)),
+            fixed((tokens, slots)),
+            fixed((tokens, slots)),
+            fixed((tokens, slots)),
+            pl.BlockSpec((HIS_PER_STEP * LO, width_dev), lambda i: (i, 0)),
+        ],
+        out_specs=pl.BlockSpec((HIS_PER_STEP, LO), lambda i: (i, 0)),
+        scratch_shapes=[pltpu.VMEM((his * tokens, 128), jnp.float32)] * (LO // 128),
+        compiler_params=pltpu.CompilerParams(vmem_limit_bytes=58 * 2**20),
+        name="score",
+    )(grads, both // LO, both % LO, parts, decoder)
+
+
+def width_sum_kernel(part, out, mid, r1, r2, send_sem, recv_sem):
+    tensor = lax.axis_index("tensor")
+    y, core = tensor // 2, lax.rem(tensor, 2)
+    peers = ({"tensor": y * 2 + (1 - core)}, {"tensor": (1 - y) * 2 + core})
+    barrier = pltpu.get_barrier_semaphore()
+    for peer in peers:
+        pl.semaphore_signal(barrier, inc=1, device_id=peer, device_id_type=pl.DeviceIdType.MESH)
+    pl.semaphore_wait(barrier, 2)
+
+    def copy(src, dst, i):
+        return pltpu.make_async_remote_copy(
+            src_ref=src, dst_ref=dst, send_sem=send_sem.at[i], recv_sem=recv_sem.at[i],
+            device_id=peers[i], device_id_type=pl.DeviceIdType.MESH,
+        )
+
+    first = copy(part, r1, 0)
+    first.start()
+    first.wait()
+    mid[...] = part[...] + r1[...]
+    second = copy(mid, r2, 1)
+    second.start()
+    second.wait()
+    out[...] = mid[...] + r2[...]
+
+
+def width_sum(part):
+    buffer = pltpu.VMEM(part.shape, part.dtype)
+    return pl.pallas_call(
+        width_sum_kernel,
+        out_shape=jax.ShapeDtypeStruct(part.shape, part.dtype),
+        in_specs=[pl.BlockSpec(memory_space=pltpu.VMEM)],
+        out_specs=pl.BlockSpec(memory_space=pltpu.VMEM),
+        scratch_shapes=[buffer] * 3 + [pltpu.SemaphoreType.DMA((2,))] * 2,
+        compiler_params=pltpu.CompilerParams(collective_id=1, has_side_effects=True),
+        name="width_sum",
+    )(part)
+
+
+def on_device_pairs(
+    cotangent,
+    resid_in,
+    gate_pre,
+    up_pre,
+    w_gate,
+    w_up,
+    w_down,
+    norm_gain,
+    decoder,
+    latent_ids,
+    latent_vals,
+    attention_mask,
+):
+    grads = chain(
+        cotangent, resid_in[0], gate_pre[0], up_pre[0], w_gate[0], w_up[0], w_down[0], norm_gain
+    )
+    lat_dev = decoder.shape[1]
+    local_ix = latent_ids[0] - lax.axis_index("feat") * lat_dev
+    inside = (local_ix >= 0) & (local_ix < lat_dev)
+    live = attention_mask.astype(jnp.float32)
+    weights = jnp.where(inside, latent_vals[0] * live[:, None], 0.0)
+    slot_ix = jnp.clip(local_ix, 0, lat_dev - 1)
+    return width_sum(score(grads, decoder[0], slot_ix, weights)).reshape(1, lat_dev)
+
+
 def solution(mesh):
+    in_pairs = mesh.shape["tensor"] == 4 and mesh.shape["feat"] == 2
+    body = on_device_pairs if in_pairs else on_device
     return jax.shard_map(
-        on_device,
+        body,
         mesh=mesh,
         in_specs=(
             P("feat", "tensor"),

time: 746 us -> 249 us (0.33); the launches traced: 737 us -> 249 us
  waiting for transfers between devices: 431 us -> 0 us
  Pallas kernels: 0 us -> 243 us
  matrix products: 118 us -> 0 us
  blocking collectives: 64.3 us -> 0 us
  other arithmetic: 66.7 us -> 2.44 us
  local copies, waits for them, and re-layouts: 37.9 us -> 3.4 us
  between operations: 14.1 us -> 0.04 us
    psum x5 -> x0, waiting for transfers between devices: 341 us -> none  [the longest x4 309 us: layer_backward(): hidden_grad = lax.psum(partial_hidden, 'tensor')]
    pallas_call x0 -> x3, Pallas kernels: none -> 243 us  [the longest x1 171 us: chain(): pl.pallas_call(functools.partial(chain_kernel, pieces, width), out_shape=...]
    dot_general x13 -> x0, matrix products: 118 us -> none  [the longest x4 32.1 us: layer_backward(): lax.dot_general(gate_grad, w_gate, (((1,), (1,)), ((), ())), preferred_el...]
    reduce_scatter x4 -> x0, waiting for transfers between devices: 57.2 us -> none  [layer_backward(): lax.psum_scatter(first + second, 'feat', scatter_dimension=0, tiled=True)]
    unnamed x5 -> x0, other arithmetic: 56.9 us -> none
    all_gather x5 -> x0, blocking collectives: 37.9 us -> none  [the longest x4 28.4 us: layer_backward(): lax.all_gather(result.astype(jnp.bfloat16), 'feat', axis=0, tiled=True)]
    scatter-add x1 -> x0, local copies, waits for them, and re-layouts: 35.9 us -> none  [on_device(): jnp.zeros((tokens, lat_dev), jnp.float32).at[token_ix, slot_ix]]
    ppermute x3 -> x0, waiting for transfers between devices: 32.3 us -> none  [passed_along(): lax.ppermute(value, axis, [(source, source + steps) for source in range(f...]
  transfers between devices with their start and end apart: 12 -> 0, of which waited for: 11 -> 0; matrix products, arithmetic and copies ran while one was open for 13% -> 0% of each run, Pallas kernels for 0% -> 0%
where the time goes in v1:
time: 249 us
  Pallas kernels  243 us (98%)
  local copies, waits for them, and re-layouts  3.4 us (1%)
    pallas_call x1, Pallas kernels, chain(): pl.pallas_call(functools.partial(chain_kernel, pieces, width), out_shape=...  171 us
    pallas_call x1, Pallas kernels, score(): pl.pallas_call(score_kernel, grid=(his // HIS_PER_STEP,), out_shape=jax.S...  63.1 us
    pallas_call x1, Pallas kernels, width_sum(): pl.pallas_call(width_sum_kernel, out_shape=jax.ShapeDtypeStruct(part.shap...  8.63 us

profile of v1, /device:TPU:0, one launch (start us, length us, event | category | flops | bytes accessed | tf_op | source)
XLA Modules:
  0.0 248.6 jit_solution(10438780302581192127)
XLA Ops:
  0.0 0.7 convert_element_type.9
  0.7 0.9 copy.13
  1.6 0.9 copy.14
  2.4 0.1 convert_convert_fusion
  2.5 0.7 pad_maximum_fusion.weights
  3.3 0.9 add_select_fusion
  4.2 171.0 %chain.1.grads = bf16[256,896]{1,0:T(8,128)(2,1)} custom-call(bf16[128,896]{1,0:T(8,128)(2,1)} %cot.1, bf16[128,896]{1,0:T(8,128)(2,1)} %bitcast.33, bf16[256,3584]{1,0:T(8,128)(2,1)} %bitcast.30, bf16[256,3584]{1,0:T(8,128)(2,1)} %bitcast.31, bf16[896,3584]{1,0:T(8,128)(2,1)} %bitcast.27, bf16[896,3584]{1,0:T(8,128)(2,1)} %bitcast.28, ...), custom_call_target="tpu_custom_call" | custom-call | tf_op jit(solution)/shard_map/chain/pallas_call | solution.py:418
  175.2 63.1 %score.1.part = f32[128,256]{1,0:T(8,128)} custom-call(bf16[256,896]{1,0:T(8,128)(2,1)} %chain.1.grads, s32[256,64]{1,0:T(8,128)} %get-tuple-element.8.hi_ids, s32[256,64]{1,0:T(8,128)} %get-tuple-element.7.lo_ids, f32[256,64]{1,0:T(8,128)} %pad_maximum_fusion.weights, bf16[32768,896]{1,0:T(8,128)(2,1)} %bitcast.26), custom_call_target="tpu_custom_call" | custom-call | tf_op jit(solution)/shard_map/score/pallas_call | solution.py:488
  238.3 8.6 %width_sum.1 = f32[128,256]{1,0:T(8,128)} custom-call(f32[128,256]{1,0:T(8,128)} %score.1.part), custom_call_target="tpu_custom_call" | custom-call | tf_op jit(solution)/shard_map/width_sum/pallas_call | solution.py:533
  246.9 1.7 copy.15
  (1 shorter events, 0.0 us)

commit v2 on v1

--- a/solution.py
+++ b/solution.py
@@ -264,7 +264,7 @@
     def _():
         pl.loop(0, pieces)(factors)
 
-    tile = 256
+    tile = half // 2
 
     def first_matmul(p):
         @pl.when(jnp.logical_not(is_top) | (p // own_pieces != feat))
@@ -309,7 +309,7 @@
 
     def second_matmul(p):
         ag_arrival(p).wait_recv()
-        part = 512
+        part = half
         nacc[rows_of(p), :] = jnp.zeros((rows, nacc.shape[1]), jnp.float32)
 
         @pl.loop(0, ff // part)
@@ -448,12 +448,13 @@
     )(cotangent, resid, gate, upper, wg, wu, wd, gain)
 
 
-def score_kernel(grads, hi_ids, lo_ids, weights, dec, out, *dense):
-    tokens = grads.shape[0]
-    his = dense[0].shape[0] // tokens
-    slots = hi_ids.shape[1]
-
-    @pl.when(pl.program_id(0) == 0)
+def acts_kernel(early, hi_ids, lo_ids, weights, *refs):
+    out, left, right, stage, sem = refs[-5:]
+    tokens, slots = hi_ids.shape
+    his = left.shape[0] // tokens
+    is_early = lax.axis_index("pipe") < lax.axis_size("pipe") - 2
+
+    @pl.when(is_early if early else jnp.logical_not(is_early))
     def _():
         @pl.loop(0, tokens, unroll=4)
         def _(t):
@@ -463,44 +464,78 @@
             lhs = jnp.where(hi, weights[at, :], 0.0).astype(jnp.bfloat16)
             rhs = jnp.where(lo, 1.0, 0.0).astype(jnp.bfloat16)
             value = lax.dot_general(lhs, rhs, NT, preferred_element_type=jnp.float32)
-            for n, ref in enumerate(dense):
-                ref[pl.ds(t, his, stride=tokens), :] = value[:, n * 128 : (n + 1) * 128]
-
-    first = pl.program_id(0) * HIS_PER_STEP
+            left[pl.ds(t, his, stride=tokens), :] = value[:, :128]
+            right[pl.ds(t, his, stride=tokens), :] = value[:, 128:]
+
+        block = stage.shape[1]
+
+        def copy(n):
+            slot = lax.rem(n, 2)
+            at = pl.ds(pl.multiple_of(n * block, block), block)
+            return pltpu.make_async_copy(stage.at[slot], out.at[at], sem.at[slot])
+
+        steps = his * tokens // block
+
+        @pl.loop(0, steps)
+        def _(n):
+            @pl.when(n >= 2)
+            def _():
+                copy(n - 2).wait()
+
+            at = pl.ds(pl.multiple_of(n * block, block), block)
+            stage[lax.rem(n, 2), :, 0:128] = left[at, :].astype(jnp.bfloat16)
+            stage[lax.rem(n, 2), :, 128:256] = right[at, :].astype(jnp.bfloat16)
+            copy(n).start()
+
+        copy(steps - 2).wait()
+        copy(steps - 1).wait()
+
+
+def build_acts(his, both, parts, *before):
+    early = not before
+    tokens = both.shape[0]
+    block = HIS_PER_STEP * tokens
+    in_vmem = pl.BlockSpec(memory_space=pltpu.VMEM)
+    anywhere = pl.BlockSpec(memory_space=pl.ANY)
+    return pl.pallas_call(
+        functools.partial(acts_kernel, early),
+        out_shape=jax.ShapeDtypeStruct((his * tokens, LO), jnp.bfloat16),
+        in_specs=[in_vmem] * 3 + [anywhere] * len(before),
+        out_specs=anywhere,
+        input_output_aliases={3: 0} if before else {},
+        scratch_shapes=[pltpu.VMEM((his * tokens, 128), jnp.float32)] * 2
+        + [pltpu.VMEM((2, block, LO), jnp.bfloat16), pltpu.SemaphoreType.DMA((2,))],
+        compiler_params=pltpu.CompilerParams(vmem_limit_bytes=58 * 2**20),
+        name="acts_early" if early else "acts_late",
+    )(both // LO, both % LO, parts, *before)
+
+
+def score_kernel(grads, acts, dec, out):
+    tokens = grads.shape[0]
     for j in range(HIS_PER_STEP):
         scores = lax.dot_general(
             grads[...], dec[j * LO : (j + 1) * LO, :], NT, preferred_element_type=jnp.float32
         )
-        at = pl.ds(pl.multiple_of((first + j) * tokens, tokens), tokens)
-        for n, ref in enumerate(dense):
-            cols = slice(n * 128, (n + 1) * 128)
-            out[j : j + 1, cols] = jnp.sum(ref[at, :] * scores[:, cols], axis=0, keepdims=True)
-
-
-def score(grads, decoder, ids, weights):
+        own = acts[j * tokens : (j + 1) * tokens, :].astype(jnp.float32)
+        out[j : j + 1, :] = jnp.sum(own * scores, axis=0, keepdims=True)
+
+
+def score(grads, decoder, acts):
     tokens, width_dev = grads.shape
     his = decoder.shape[0] // LO
-    coarse = weights.astype(jnp.bfloat16).astype(jnp.float32)
-    parts = jnp.concatenate([coarse, weights - coarse], axis=1)
-    both = jnp.concatenate([ids, ids], axis=1)
-    slots = both.shape[1]
-    fixed = lambda shape: pl.BlockSpec(shape, lambda i: (0, 0))
     return pl.pallas_call(
         score_kernel,
         grid=(his // HIS_PER_STEP,),
         out_shape=jax.ShapeDtypeStruct((his, LO), jnp.float32),
         in_specs=[
-            fixed((tokens, width_dev)),
-            fixed((tokens, slots)),
-            fixed((tokens, slots)),
-            fixed((tokens, slots)),
+            pl.BlockSpec((tokens, width_dev), lambda i: (0, 0)),
+            pl.BlockSpec((HIS_PER_STEP * tokens, LO), lambda i: (i, 0)),
             pl.BlockSpec((HIS_PER_STEP * LO, width_dev), lambda i: (i, 0)),
         ],
         out_specs=pl.BlockSpec((HIS_PER_STEP, LO), lambda i: (i, 0)),
-        scratch_shapes=[pltpu.VMEM((his * tokens, 128), jnp.float32)] * (LO // 128),
-        compiler_params=pltpu.CompilerParams(vmem_limit_bytes=58 * 2**20),
+        compiler_params=pltpu.CompilerParams(vmem_limit_bytes=40 * 2**20),
         name="score",
-    )(grads, both // LO, both % LO, parts, decoder)
+    )(grads, acts, decoder)
 
 
 def width_sum_kernel(part, out, mid, r1, r2, send_sem, recv_sem):
@@ -555,16 +590,24 @@
     latent_vals,
     attention_mask,
 ):
-    grads = chain(
-        cotangent, resid_in[0], gate_pre[0], up_pre[0], w_gate[0], w_up[0], w_down[0], norm_gain
-    )
     lat_dev = decoder.shape[1]
     local_ix = latent_ids[0] - lax.axis_index("feat") * lat_dev
     inside = (local_ix >= 0) & (local_ix < lat_dev)
     live = attention_mask.astype(jnp.float32)
     weights = jnp.where(inside, latent_vals[0] * live[:, None], 0.0)
     slot_ix = jnp.clip(local_ix, 0, lat_dev - 1)
-    return width_sum(score(grads, decoder[0], slot_ix, weights)).reshape(1, lat_dev)
+    coarse = weights.astype(jnp.bfloat16).astype(jnp.float32)
+    parts = jnp.concatenate([coarse, weights - coarse], axis=1)
+    both = jnp.concatenate([slot_ix, slot_ix], axis=1)
+    his = lat_dev // LO
+    acts = build_acts(his, both, parts)
+    acts, cotangent = lax.optimization_barrier((acts, cotangent))
+    grads = chain(
+        cotangent, resid_in[0], gate_pre[0], up_pre[0], w_gate[0], w_up[0], w_down[0], norm_gain
+    )
+    acts, grads = lax.optimization_barrier((acts, grads))
+    acts = build_acts(his, both, parts, acts)
+    return width_sum(score(grads, decoder[0], acts)).reshape(1, lat_dev)
 
 
 def solution(mesh):

time: 249 us -> 220 us (0.88)
  Pallas kernels: 243 us -> 213 us
    pallas_call x0 -> x2, Pallas kernels: none -> 44.9 us  [build_acts(): pl.pallas_call(functools.partial(acts_kernel, early), out_shape=jax.Shape...]
    pallas_call x1, Pallas kernels: 171 us -> 127 us  [chain(): pl.pallas_call(functools.partial(chain_kernel, pieces, width), out_shape=...]
    pallas_call x1, Pallas kernels: 63.1 us -> 31.9 us  [score(): pl.pallas_call(score_kernel, grid=(his // HIS_PER_STEP,), out_shape=jax.S...]
where the time goes in v2:
time: 220 us
  Pallas kernels  213 us (97%)
  local copies, waits for them, and re-layouts  4.14 us (2%)
  other arithmetic  2.45 us (1%)
    pallas_call x1, Pallas kernels, chain(): pl.pallas_call(functools.partial(chain_kernel, pieces, width), out_shape=...  127 us
    pallas_call x2, Pallas kernels, build_acts(): pl.pallas_call(functools.partial(acts_kernel, early), out_shape=jax.Shape...  44.9 us
    pallas_call x1, Pallas kernels, score(): pl.pallas_call(score_kernel, grid=(his // HIS_PER_STEP,), out_shape=jax.S...  31.9 us
    pallas_call x1, Pallas kernels, width_sum(): pl.pallas_call(width_sum_kernel, out_shape=jax.ShapeDtypeStruct(part.shap...  8.64 us

profile of v2, /device:TPU:0, one launch (start us, length us, event | category | flops | bytes accessed | tf_op | source)
XLA Modules:
  0.0 219.6 jit_solution(13664087956201273669)
XLA Ops:
  0.0 0.7 convert_element_type.9
  0.7 0.9 copy.14
  1.6 0.9 copy.15
  2.4 0.1 convert_convert_fusion
  2.5 0.7 pad_maximum_fusion.weights
  3.3 0.9 add_select_fusion
  4.2 43.8 %acts_early.1.refs_0_ = bf16[32768,256]{1,0:T(8,128)(2,1)} custom-call(s32[256,64]{1,0:T(8,128)} %get-tuple-element.16.hi_ids, s32[256,64]{1,0:T(8,128)} %get-tuple-element.15.lo_ids, f32[256,64]{1,0:T(8,128)} %pad_maximum_fusion.weights), custom_call_target="tpu_custom_call" | custom-call | tf_op jit(solution)/shard_map/acts_early/pallas_call | solution.py:500
  48.0 127.5 %chain.1.grads = bf16[256,896]{1,0:T(8,128)(2,1)} custom-call(bf16[128,896]{1,0:T(8,128)(2,1)} %cot, bf16[128,896]{1,0:T(8,128)(2,1)} %bitcast.33, bf16[256,3584]{1,0:T(8,128)(2,1)} %bitcast.30, bf16[256,3584]{1,0:T(8,128)(2,1)} %bitcast.31, bf16[896,3584]{1,0:T(8,128)(2,1)} %bitcast.27, bf16[896,3584]{1,0:T(8,128)(2,1)} %bitcast.28, ...), custom_call_target="tpu_custom_call" | custom-call | tf_op jit(solution)/shard_map/chain/pallas_call | solution.py:418
  175.5 0.0 copy-start
  175.5 1.1 acts_late.1.acts
  176.6 0.1 copy-done
  176.7 31.9 %score.1.part = f32[128,256]{1,0:T(8,128)S(1)} custom-call(bf16[256,896]{1,0:T(8,128)(2,1)S(1)} %copy-done, bf16[32768,256]{1,0:T(8,128)(2,1)} %acts_late.1.acts, bf16[32768,896]{1,0:T(8,128)(2,1)} %bitcast.26), custom_call_target="tpu_custom_call" | custom-call | tf_op jit(solution)/shard_map/score/pallas_call | solution.py:526
  208.6 0.0 copy-start.1
  208.6 0.6 copy-done.1
  209.3 8.6 %width_sum.1 = f32[128,256]{1,0:T(8,128)} custom-call(f32[128,256]{1,0:T(8,128)} %copy-done.1), custom_call_target="tpu_custom_call" | custom-call | tf_op jit(solution)/shard_map/width_sum/pallas_call | solution.py:568
  217.9 1.7 copy.16
  (1 shorter events, 0.0 us)
Async XLA Ops:
  175.5 1.2 copy-start
  208.6 0.7 copy-start.1
